TPU v7x, 32 devices: a whole 2x2x4 slice. The times are simulated.
32 devices in a mesh: group: 2 (over x), gx: 16 (over z, y, core).
Axes of the slice: x: 2, y: 2, z: 4, core: 2. Of those that a mesh axis runs over, the one named last changes fastest.
Arguments:
- tokens: bfloat16 [8192, 768], P('gx', 'group'), parts along dimension 1, may hold values from -190 to 190, as said below
- norm_gain: bfloat16 [8192], P('gx'), may hold values from 0.099609375 to 1.8984375
- gate_weight: bfloat16 [16, 2048, 8192], P('gx'), may hold values from -0.0625 to 0.0625
- up_weight: bfloat16 [16, 2048, 8192], P('gx'), may hold values from -0.0625 to 0.0625
- down_weight: bfloat16 [16, 8192, 2048], P('gx'), may hold values from -0.03125 to 0.03125
Outputs:
- output: bfloat16 [8192, 768], P('gx', 'group'), parts along dimension 1
There are 2 independent parts, one for each index of `group`. A program takes and returns all parts, laid end to end along the dimension named above; an argument that names none is the same for every part. Nothing has to cross between parts.
Inputs may be any that keep to these rules, and one draw needn't show every extreme that they name: `tokens`: activations of a batch.
All inputs are finite; a program needn't handle non-finite values.
Results may differ from a plain program's by a relative error of at most 0.0065.
Values may be sent and summed in bfloat16 or wider, within the bound.
A program may use at most 320 MiB of HBM per device.

v0:
```python
import jax
import jax.numpy as jnp
from jax import lax
from jax.sharding import PartitionSpec as P

D = 8192
GA = 4


def partner(shard, axis, stride):
    return lax.ppermute(shard, axis, [(i, i ^ 1 << stride) for i in range(lax.axis_size(axis))])


def pair_join(piece, other, flag):
    first = jnp.where(flag, other, piece)
    second = jnp.where(flag, piece, other)
    return jnp.concatenate([first, second], axis=0)


def halve(value, flag):
    middle = value.shape[0] // 2
    lower = value[:middle]
    upper = value[middle:]
    return (jnp.where(flag, upper, lower), jnp.where(flag, lower, upper))


def shards(tokens, norm_gain, gate_weight, up_weight, down_weight):
    contract = (((0,), (0,)), ((), ()))
    count = lax.axis_size("gx")
    blocks = count // GA
    low_digits = blocks.bit_length() - 1
    high_digits = GA.bit_length() - 1
    position = lax.axis_index("gx")

    def bit_set(bit):
        return position >> bit & 1 == 1

    values = tokens.astype(jnp.float32)
    squares = lax.psum(jnp.sum(values * values, axis=0), "gx")
    inverse = lax.rsqrt(squares / D + 1e-05)
    normed = (values * inverse[None, :] * norm_gain.astype(jnp.float32)[:, None]).astype(
        jnp.bfloat16
    )
    piece = normed
    for bit in range(low_digits):
        other = partner(piece, "gx", bit)
        piece = pair_join(piece, other, bit_set(bit))
    gate_part = lax.dot_general(gate_weight[0], piece, contract, preferred_element_type=jnp.float32)
    up_part = lax.dot_general(up_weight[0], piece, contract, preferred_element_type=jnp.float32)
    for step in range(high_digits):
        bit = low_digits + step
        gate_got, up_got = partner((gate_part, up_part), "gx", bit)
        gate_part = gate_part + gate_got
        up_part = up_part + up_got
    hidden = (jax.nn.silu(gate_part) * up_part).astype(jnp.bfloat16)
    partial_value = lax.dot_general(
        down_weight[0], hidden, contract, preferred_element_type=jnp.float32
    )
    for step in range(low_digits):
        bit = low_digits - 1 - step
        kept, sent = halve(partial_value, bit_set(bit))
        partial_value = kept + partner(sent, "gx", bit)
    return partial_value.astype(jnp.bfloat16)


def solution(mesh):
    placed = (
        P("gx", "group"),
        P("gx"),
        P("gx", None, None),
        P("gx", None, None),
        P("gx", None, None),
    )
    return jax.shard_map(
        shards, mesh=mesh, in_specs=placed, out_specs=P("gx", "group"), check_vma=False
    )
```

profile of v0, /device:TPU:0, one launch (start us, length us, event | category | flops | bytes accessed | tf_op | source)
XLA Modules:
  0.0 1508.3 jit_solution(4371182595154695862)
XLA Ops:
  0.0 0.7 convert_element_type.16
  0.7 1.2 copy.6
  1.9 0.2 fusion.16
  2.0 34.9 %psum.7 = f32[384]{0:T(512)S(1)} all-reduce(f32[384]{0:T(512)S(1)} %fusion.16), channel_id=1, replica_groups=mesh['group'=2,'gx'=16] {'gx'}, use_global_device_ids=true, to_apply=%region_1.0 | all-reduce | flops 384 | bytes 3072 | tf_op jit(solution)/shard_map/psum | solution.py:39
  36.9 0.2 fusion.18
  37.1 0.1 collective-permute-start
  37.2 1.7 collective-permute-done
  38.9 0.3 broadcast_select_fusion.3
  39.2 0.1 pad_maximum_fusion.3
  39.3 0.1 collective-permute-start.1
  39.4 19.6 %collective-permute-done.1 = bf16[1024,384]{0,1:T(8,128)(2,1)S(1)} collective-permute-done((bf16[1024,384]{0,1:T(8,128)(2,1)S(1)}, bf16[1024,384]{0,1:T(8,128)(2,1)S(1)}, u32[]{:S(2)}, u32[]{:S(2)}) %collective-permute-start.1) | collective-permute-done | bytes 786464 | tf_op jit(solution)/shard_map/ppermute | solution.py:11
  58.9 0.4 broadcast_select_fusion.1
  59.3 21.8 %fusion.6 = f32[8192,384]{0,1:T(8,128)} fusion(bf16[1,2048,8192]{2,1,0:T(8,128)(2,1)} %param.7, bf16[1024,384]{0,1:T(8,128)(2,1)S(1)} %get-tuple-element.6, bf16[1024,384]{0,1:T(8,128)(2,1)S(1)} %get-tuple-element.5), kind=kOutput, calls=%fused_computation.7 | convolution fusion | flops 12888047616 | bytes 47710208 | tf_op jit(solution)/shard_map/dot_general | solution.py:48
  81.1 0.0 collective-permute-start.2
  81.1 21.7 %fusion.9 = f32[8192,384]{0,1:T(8,128)} fusion(bf16[1,2048,8192]{2,1,0:T(8,128)(2,1)} %param.8, bf16[1024,384]{0,1:T(8,128)(2,1)S(1)} %get-tuple-element.6, bf16[1024,384]{0,1:T(8,128)(2,1)S(1)} %get-tuple-element.5), kind=kOutput, calls=%fused_computation.8 | convolution fusion | flops 12888047616 | bytes 47710208 | tf_op jit(solution)/shard_map/dot_general | solution.py:49
  102.8 0.0 copy-start.1
  102.8 2.0 collective-permute-start.4
  104.8 249.9 %collective-permute-done.2 = f32[8192,384]{0,1:T(8,128)} collective-permute-done((f32[8192,384]{0,1:T(8,128)}, f32[8192,384]{0,1:T(8,128)}, u32[]{:S(2)}, u32[]{:S(2)}) %collective-permute-start.2) | collective-permute-done | bytes 12582944 | tf_op jit(solution)/shard_map/ppermute | solution.py:11
  354.7 8.9 add.32
  363.7 0.0 copy-start
  363.7 0.1 collective-permute-start.3
  363.8 514.9 %collective-permute-done.4 = f32[8192,384]{0,1:T(8,128)} collective-permute-done((f32[8192,384]{0,1:T(8,128)}, f32[8192,384]{0,1:T(8,128)}, u32[]{:S(2)}, u32[]{:S(2)}) %collective-permute-start.4) | collective-permute-done | bytes 12582944 | tf_op jit(solution)/shard_map/ppermute | solution.py:11
  878.7 0.0 copy-done.1
  878.7 10.5 add.35
  889.2 0.0 copy-done
  889.2 1.6 collective-permute-start.5
  890.8 286.6 %collective-permute-done.3 = f32[8192,384]{0,1:T(8,128)} collective-permute-done((f32[8192,384]{0,1:T(8,128)S(1)}, f32[8192,384]{0,1:T(8,128)}, u32[]{:S(2)}, u32[]{:S(2)}) %collective-permute-start.3) | collective-permute-done | bytes 12582944 | tf_op jit(solution)/shard_map/ppermute | solution.py:11
  1177.3 265.3 %collective-permute-done.5 = f32[8192,384]{0,1:T(8,128)} collective-permute-done((f32[8192,384]{0,1:T(8,128)}, f32[8192,384]{0,1:T(8,128)}, u32[]{:S(2)}, u32[]{:S(2)}) %collective-permute-start.5) | collective-permute-done | bytes 12582944 | tf_op jit(solution)/shard_map/ppermute | solution.py:11
  1442.6 28.9 %fusion.13 = f32[2048,384]{0,1:T(8,128)S(1)} fusion(bf16[1,8192,2048]{2,1,0:T(8,128)(2,1)} %param.9, f32[8192,384]{0,1:T(8,128)} %add.35, f32[8192,384]{0,1:T(8,128)} %collective-permute-done.5, f32[8192,384]{0,1:T(8,128)} %copy-done, f32[8192,384]{0,1:T(8,128)} %collective-permute-done.3), kind=kOutput, calls=%fused_computation.10 | convolution fusion | flops 12910067712 | bytes 87031808 | tf_op jit(solution)/shard_map/dot_general | solution.py:56
  1471.5 0.3 slice_select_fusion
  1471.8 1.0 collective-permute-start.6
  1472.9 31.1 %collective-permute-done.6 = f32[1024,384]{0,1:T(8,128)S(1)} collective-permute-done((f32[1024,384]{0,1:T(8,128)S(1)}, f32[1024,384]{0,1:T(8,128)S(1)}, u32[]{:S(2)}, u32[]{:S(2)}) %collective-permute-start.6) | collective-permute-done | bytes 1572896 | tf_op jit(solution)/shard_map/ppermute | solution.py:11
  1504.0 0.6 select_add_fusion
  1504.6 0.1 slice_select_fusion.1
  1504.7 0.1 collective-permute-start.7
  1504.8 2.3 collective-permute-done.7
  1507.1 0.3 add_convert_fusion
  1507.4 0.9 copy.7
  (1 shorter events, 0.0 us)
Async XLA Ops:
  37.1 1.8 collective-permute-start
  39.3 19.6 %collective-permute-start.1 = (bf16[1024,384]{0,1:T(8,128)(2,1)S(1)}, bf16[1024,384]{0,1:T(8,128)(2,1)S(1)}, u32[]{:S(2)}, u32[]{:S(2)}) collective-permute-start(bf16[1024,384]{0,1:T(8,128)(2,1)S(1)} %pad_maximum_fusion.3), channel_id=1, source_target_pairs={{0,2},{1,3},{2,0},{3,1},{4,6},{5,7},{6,4},{7,5},{8,10},{9,11},{10,... | collective-permute-start | bytes 2359304 | tf_op jit(solution)/shard_map/ppermute | solution.py:11
  81.1 273.6 %collective-permute-start.2 = (f32[8192,384]{0,1:T(8,128)}, f32[8192,384]{0,1:T(8,128)}, u32[]{:S(2)}, u32[]{:S(2)}) collective-permute-start(f32[8192,384]{0,1:T(8,128)} %fusion.6), channel_id=1, source_target_pairs={{0,4},{1,5},{2,6},{3,7},{4,0},{5,1},{6,2},{7,3},{8,12},{9,13},{10,... | collective-permute-start | bytes 37748744 | tf_op jit(solution)/shard_map/ppermute | solution.py:11
  102.8 775.9 %copy-start.1 = (f32[8192,384]{0,1:T(8,128)S(1)}, f32[8192,384]{0,1:T(8,128)}, u32[]{:S(2)}) copy-start(f32[8192,384]{0,1:T(8,128)} %fusion.9) | copy-start | bytes 37748740
  102.8 775.8 %collective-permute-start.4 = (f32[8192,384]{0,1:T(8,128)}, f32[8192,384]{0,1:T(8,128)}, u32[]{:S(2)}, u32[]{:S(2)}) collective-permute-start(f32[8192,384]{0,1:T(8,128)} %fusion.9), channel_id=1, source_target_pairs={{0,4},{1,5},{2,6},{3,7},{4,0},{5,1},{6,2},{7,3},{8,12},{9,13},{10,... | collective-permute-start | bytes 37748744 | tf_op jit(solution)/shard_map/ppermute | solution.py:11
  363.7 525.5 %copy-start = (f32[8192,384]{0,1:T(8,128)}, f32[8192,384]{0,1:T(8,128)S(1)}, u32[]{:S(2)}) copy-start(f32[8192,384]{0,1:T(8,128)S(1)} %add.32) | copy-start | bytes 37748740
  363.7 813.6 %collective-permute-start.3 = (f32[8192,384]{0,1:T(8,128)S(1)}, f32[8192,384]{0,1:T(8,128)}, u32[]{:S(2)}, u32[]{:S(2)}) collective-permute-start(f32[8192,384]{0,1:T(8,128)S(1)} %add.32), channel_id=1, source_target_pairs={{0,8},{1,9},{2,10},{3,11},{4,12},{5,13},{6,14},{7,15},{8,0},{9,1},... | collective-permute-start | bytes 37748744 | tf_op jit(solution)/shard_map/ppermute | solution.py:11
  889.2 553.5 %collective-permute-start.5 = (f32[8192,384]{0,1:T(8,128)}, f32[8192,384]{0,1:T(8,128)}, u32[]{:S(2)}, u32[]{:S(2)}) collective-permute-start(f32[8192,384]{0,1:T(8,128)} %add.35), channel_id=1, source_target_pairs={{0,8},{1,9},{2,10},{3,11},{4,12},{5,13},{6,14},{7,15},{8,0},{9,1},... | collective-permute-start | bytes 37748744 | tf_op jit(solution)/shard_map/ppermute | solution.py:11
  1471.8 32.1 %collective-permute-start.6 = (f32[1024,384]{0,1:T(8,128)S(1)}, f32[1024,384]{0,1:T(8,128)S(1)}, u32[]{:S(2)}, u32[]{:S(2)}) collective-permute-start(f32[1024,384]{0,1:T(8,128)S(1)} %slice_select_fusion), channel_id=1, source_target_pairs={{0,2},{1,3},{2,0},{3,1},{4,6},{5,7},{6,4},{7,5},{8,10},{9,11},{10,... | collective-permute-start | bytes 4718600 | tf_op jit(solution)/shard_map/ppermute | solution.py:11
  1504.7 2.4 collective-permute-start.7
where the time goes:
time: 1510 us
  waiting for transfers between devices  1370 us (91%)
  matrix products  72.4 us (5%)
  blocking collectives  34.9 us (2%)
  other arithmetic  22.5 us (1%)
    ppermute x8, waiting for transfers between devices, partner(): lax.ppermute(shard, axis, [(i, i ^ 1 << stride) for i in range(lax.axis_s...  1370 us
    psum x1, blocking collectives, shards(): squares = lax.psum(jnp.sum(values * values, axis=0), 'gx')  34.9 us
  transfers between devices with their start and end apart: 8, of which 8 were waited for; matrix products, arithmetic and copies ran while one was open for 3% of the time, Pallas kernels for 0%

commit v1 on v0

v1 whole, which is shorter than its diff:
```python
import functools

import jax
import jax.numpy as jnp
from jax import lax
from jax.experimental import pallas as pl
from jax.experimental.pallas import tpu as pltpu
from jax.sharding import PartitionSpec as P

GA = 4
CHUNK = 128
SKEW = 2
F32 = jnp.float32
BF16 = jnp.bfloat16


def kernel(
    count,
    tok_ref,
    gain_ref,
    gate_ref,
    up_ref,
    down_ref,
    out_ref,
    ssq,
    gath,
    norm_t,
    part,
    red,
    hid,
    wgu,
    wdn,
    acc,
    final,
    send_buf,
    recv_buf,
    sq_send,
    sq_recv,
    ga_send,
    ga_recv,
    red_send,
    red_recv,
    hid_send,
    hid_recv,
    wg_sem,
    wu_sem,
    wd_sem,
    fin_send,
    fin_recv,
):
    blocks = count // GA
    shard, rows = tok_ref.shape
    width = shard * blocks
    units = gate_ref.shape[2]
    half = units // 2
    steps = half // CHUNK
    last = GA - 1
    me = lax.axis_index("gx")
    a = me // blocks
    b = me % blocks

    def remote(src, dst, send, recv, to):
        return pltpu.make_async_remote_copy(
            src_ref=src,
            dst_ref=dst,
            send_sem=send,
            recv_sem=recv,
            device_id={"gx": to},
            device_id_type=pl.DeviceIdType.MESH,
        )

    roles = (a, last - a)
    nexts = (me + blocks, me - blocks)
    prevs = (me - blocks, me + blocks)

    def wide_copies(d, k, slot):
        cols = pl.ds(pl.multiple_of(d * half + k * CHUNK, CHUNK), CHUNK)
        return (
            pltpu.make_async_copy(
                gate_ref.at[0, :, cols], wgu.at[d, slot, :, pl.ds(0, CHUNK)], wg_sem.at[d, slot]
            ),
            pltpu.make_async_copy(
                up_ref.at[0, :, cols], wgu.at[d, slot, :, pl.ds(CHUNK, CHUNK)], wu_sem.at[d, slot]
            ),
        )

    def down_copy(d, k, slot):
        lines = pl.ds(pl.multiple_of(d * half + k * CHUNK, CHUNK), CHUNK)
        return pltpu.make_async_copy(down_ref.at[0, lines, :], wdn.at[d, slot], wd_sem.at[d, slot])

    def red_copy(d, k):
        slot = red.at[d, k]
        return remote(slot, slot, red_send.at[d, k], red_recv.at[d, k], nexts[d])

    def hid_copy(d, k):
        slot = hid.at[d, k]
        return remote(slot, slot, hid_send.at[d, k], hid_recv.at[d, k], prevs[d])

    barrier = pltpu.get_barrier_semaphore()

    @pl.loop(1, count)
    def _(j):
        pl.semaphore_signal(
            barrier,
            inc=1,
            device_id={"gx": (me + j) % count},
            device_id_type=pl.DeviceIdType.MESH,
        )

    for d in range(2):
        for copy in wide_copies(d, 0, 0):
            copy.start()
        down_copy(d, 0, 0).start()

    values = tok_ref[...].astype(F32)
    ssq[me] = jnp.sum((values * values).reshape(shard // 8, 8, rows), axis=0)
    pl.semaphore_wait(barrier, count - 1)

    def sq_copy(owner, to):
        return remote(ssq.at[owner], ssq.at[owner], sq_send.at[to], sq_recv.at[owner], to)

    @pl.loop(1, count)
    def _(j):
        sq_copy(me, (me + j) % count).start()

    @pl.loop(1, count)
    def _(j):
        other = (me + j) % count
        sq_copy(other, other).wait_recv()

    squares = jnp.sum(jnp.sum(ssq[...], axis=0), axis=0, keepdims=True)
    inverse = lax.rsqrt(squares / (shard * count) + 1e-05)
    normed = (values * inverse * gain_ref[...].astype(F32)).astype(BF16)

    def lines_of(index):
        return pl.ds(pl.multiple_of(index * shard, shard), shard)

    gath[lines_of(b), :] = normed

    def gath_copy(owner, to):
        lines = gath.at[lines_of(owner), :]
        return remote(lines, lines, ga_send.at[to], ga_recv.at[owner], a * blocks + to)

    @pl.loop(1, blocks)
    def _(j):
        gath_copy(b, (b + j) % blocks).start()

    acc[...] = jnp.zeros_like(acc)

    @pl.loop(1, count)
    def _(j):
        sq_copy(me, (me + j) % count).wait_send()

    @pl.loop(1, blocks)
    def _(j):
        other = (b + j) % blocks
        gath_copy(other, other).wait_recv()

    @pl.loop(1, blocks)
    def _(j):
        gath_copy(b, (b + j) % blocks).wait_send()

    for at in range(0, width, 256):
        norm_t[:, at : at + 256] = gath[at : at + 256, :].T

    @pl.loop(0, steps + 2 * last * SKEW)
    def _(i):
        for d in range(2):
            r = roles[d]
            k = i - SKEW * (last + last - r)

            @pl.when((k >= 0) & (k < steps) & (r < last))
            def _(d=d, r=r, k=k):
                hid_copy(d, k).wait_recv()

                @pl.when(r > 0)
                def _():
                    hid_copy(d, k).start()

        for d in range(2):
            r = roles[d]
            k = i - SKEW * r

            @pl.when((k >= 0) & (k < steps))
            def _(d=d, r=r, k=k):
                slot = lax.rem(k, 2)
                for copy in wide_copies(d, k, slot):
                    copy.wait()

                @pl.when(k + 1 < steps)
                def _():
                    for copy in wide_copies(d, k + 1, 1 - slot):
                        copy.start()

                part[...] = jnp.dot(norm_t[...], wgu[d, slot], preferred_element_type=F32)

                @pl.when(r > 0)
                def _():
                    red_copy(d, k).wait_recv()

                @pl.when(r == 0)
                def _():
                    red[d, k] = part[...].astype(BF16)

                @pl.when((r > 0) & (r < last))
                def _():
                    red[d, k] = (part[...] + red[d, k].astype(F32)).astype(BF16)

                @pl.when(r < last)
                def _():
                    red_copy(d, k).start()

                @pl.when(r == last)
                def _():
                    total = part[...] + red[d, k].astype(F32)
                    gate = total[:, :CHUNK]
                    hid[d, k] = (gate / (1.0 + jnp.exp(-gate)) * total[:, CHUNK:]).astype(BF16)
                    hid_copy(d, k).start()

        for d in range(2):
            r = roles[d]
            k = i - SKEW * (last + last - r)

            @pl.when((k >= 0) & (k < steps))
            def _(d=d, r=r, k=k):
                slot = lax.rem(k, 2)
                down_copy(d, k, slot).wait()

                @pl.when(k + 1 < steps)
                def _():
                    down_copy(d, k + 1, 1 - slot).start()

                acc[...] += jnp.dot(hid[d, k], wdn[d, slot], preferred_element_type=F32)

    bits = blocks.bit_length() - 1

    def flipped(t):
        return (b >> t) & 1

    def slice_of(t, u, digit):
        return (u << (t + 1)) + digit * (1 << t) + b % (1 << t)

    def turned(index):
        if shard % 128 == 0:
            return acc[:, lines_of(index)].T
        return final[lines_of(index), :]

    if shard % 128 != 0:
        final[...] = acc[...].T

    base = 0
    for t in range(bits):
        many = blocks >> (t + 1)
        mine = flipped(t)
        partner = me + (1 - 2 * mine) * (1 << t)
        copies = []
        for u in range(many):
            index = slice_of(t, u, 1 - mine)
            source = turned(index) if t == 0 else final[lines_of(index), :]
            send_buf[base + u] = source.astype(BF16)
            copy = remote(
                send_buf.at[base + u],
                recv_buf.at[base + u],
                fin_send.at[base + u],
                fin_recv.at[base + u],
                partner,
            )
            copy.start()
            copies.append(copy)
        if t == 0 and shard % 128 == 0:
            for u in range(many):
                index = slice_of(t, u, mine)
                final[lines_of(index), :] = turned(index)
        for u, copy in enumerate(copies):
            copy.wait()
            lines = lines_of(slice_of(t, u, mine))
            final[lines, :] = final[lines, :] + recv_buf[base + u].astype(F32)
        base += many
    out_ref[...] = final[lines_of(b), :].astype(BF16)

    for d in range(2):
        r = roles[d]

        @pl.loop(0, steps)
        def _(k, d=d, r=r):
            @pl.when(r < last)
            def _():
                red_copy(d, k).wait_send()

            @pl.when(r > 0)
            def _():
                hid_copy(d, k).wait_send()


def shards(tokens, norm_gain, gate_weight, up_weight, down_weight):
    count = lax.axis_size("gx")
    blocks = count // GA
    shard, rows = tokens.shape
    width = shard * blocks
    steps = gate_weight.shape[2] // 2 // CHUNK
    dma = pltpu.SemaphoreType.DMA
    vmem = pl.BlockSpec(memory_space=pltpu.VMEM)
    hbm = pl.BlockSpec(memory_space=pl.ANY)
    return pl.pallas_call(
        functools.partial(kernel, count),
        out_shape=jax.ShapeDtypeStruct((shard, rows), BF16),
        in_specs=[vmem, vmem, hbm, hbm, hbm],
        out_specs=vmem,
        scratch_shapes=[
            pltpu.VMEM((count, 8, rows), F32),
            pltpu.VMEM((width, rows), BF16),
            pltpu.VMEM((rows, width), BF16),
            pltpu.VMEM((rows, 2 * CHUNK), F32),
            pltpu.VMEM((2, steps, rows, 2 * CHUNK), BF16),
            pltpu.VMEM((2, steps, rows, CHUNK), BF16),
            pltpu.VMEM((2, 2, width, 2 * CHUNK), BF16),
            pltpu.VMEM((2, 2, CHUNK, width), BF16),
            pltpu.VMEM((rows, width), F32),
            pltpu.VMEM((width, rows), F32),
            pltpu.VMEM((blocks - 1, shard, rows), BF16),
            pltpu.VMEM((blocks - 1, shard, rows), BF16),
            dma((count,)),
            dma((count,)),
            dma((blocks,)),
            dma((blocks,)),
            dma((2, steps)),
            dma((2, steps)),
            dma((2, steps)),
            dma((2, steps)),
            dma((2, 2)),
            dma((2, 2)),
            dma((2, 2)),
            dma((blocks - 1,)),
            dma((blocks - 1,)),
        ],
        compiler_params=pltpu.CompilerParams(
            collective_id=0, has_side_effects=True, vmem_limit_bytes=56 * 1024 * 1024
        ),
        cost_estimate=pl.CostEstimate(
            flops=6 * width * rows * gate_weight.shape[2],
            bytes_accessed=6 * width * gate_weight.shape[2],
            transcendentals=0,
        ),
    )(tokens, norm_gain[:, None], gate_weight, up_weight, down_weight)


def solution(mesh):
    placed = (
        P("gx", "group"),
        P("gx"),
        P("gx", None, None),
        P("gx", None, None),
        P("gx", None, None),
    )
    return jax.shard_map(
        shards, mesh=mesh, in_specs=placed, out_specs=P("gx", "group"), check_vma=False
    )
```

time: 1510 us -> 276 us (0.18)
  waiting for transfers between devices: 1370 us -> 0 us
  Pallas kernels: 0 us -> 273 us
  matrix products: 72.4 us -> 0 us
  blocking collectives: 34.9 us -> 0 us
  other arithmetic: 22.5 us -> 0 us
    ppermute x8 -> x0, waiting for transfers between devices: 1370 us -> none  [partner(): lax.ppermute(shard, axis, [(i, i ^ 1 << stride) for i in range(lax.axis_s...]
    pallas_call x0 -> x1, Pallas kernels: none -> 273 us  [shards(): pl.pallas_call(functools.partial(kernel, count), out_shape=jax.ShapeDtype...]
    dot_general x3 -> x0, matrix products: 72.4 us -> none  [the longest x1 28.9 us: shards(): lax.dot_general(down_weight[0], hidden, contract, preferred_element_type=...]
    psum x1 -> x0, blocking collectives: 34.9 us -> none  [shards(): squares = lax.psum(jnp.sum(values * values, axis=0), 'gx')]
    add x3 -> x0, other arithmetic: 20 us -> none  [the longest x1 10.5 us: shards(): up_part = up_part + up_got]
  transfers between devices with their start and end apart: 8 -> 0, of which waited for: 8 -> 0; matrix products, arithmetic and copies ran while one was open for 3% -> 0% of each run, Pallas kernels for 0% -> 0%
where the time goes in v1:
time: 276 us
  Pallas kernels  273 us (99%)
  local copies, waits for them, and re-layouts  3.25 us (1%)
    pallas_call x1, Pallas kernels, shards(): pl.pallas_call(functools.partial(kernel, count), out_shape=jax.ShapeDtype...  273 us

profile of v1, /device:TPU:0, one launch (start us, length us, event | category | flops | bytes accessed | tf_op | source)
XLA Modules:
  0.0 275.8 jit_solution(6948119673690650729)
XLA Ops:
  0.0 1.5 broadcast_in_dim.4.gain_ref
  1.5 272.5 %shard_map.55 = bf16[512,384]{1,0:T(8,128)(2,1)} custom-call(bf16[512,384]{1,0:T(8,128)(2,1)} %tok_ref.1, bf16[512,1]{1,0:T(8,128)(2,1)} %broadcast_in_dim.4.gain_ref, bf16[1,2048,8192]{2,1,0:T(8,128)(2,1)} %gate_ref.1, bf16[1,2048,8192]{2,1,0:T(8,128)(2,1)} %up_ref.1, bf16[1,8192,2048]{2,1,0:T(8,128)(2,1)} %down_ref.1), custom_call_target="tpu_custom_call" | custom-call | flops 38654705664 | bytes 100663296 | tf_op jit(solution)/shard_map/pallas_call | solution.py:304
  274.0 1.8 copy.8

commit v2 on v1

--- a/solution.py
+++ b/solution.py
@@ -10,6 +10,7 @@
 GA = 4
 CHUNK = 128
 SKEW = 2
+BACK = 2
 F32 = jnp.float32
 BF16 = jnp.bfloat16
 
@@ -23,6 +24,7 @@
     down_ref,
     out_ref,
     ssq,
+    gains,
     gath,
     norm_t,
     part,
@@ -36,6 +38,8 @@
     recv_buf,
     sq_send,
     sq_recv,
+    gain_send,
+    gain_recv,
     ga_send,
     ga_recv,
     red_send,
@@ -112,62 +116,90 @@
             copy.start()
         down_copy(d, 0, 0).start()
 
+    def lines_of(index):
+        return pl.ds(pl.multiple_of(index * shard, shard), shard)
+
+    bits = blocks.bit_length() - 1
+    plan = []
+    for t in reversed(range(bits)):
+        plan.append((t, (blocks >> (t + 1)) - 1, blocks >> (t + 1)))
+
+    def sq_copy(owner, to):
+        return remote(ssq.at[owner], ssq.at[owner], sq_send.at[to], sq_recv.at[owner], to)
+
+    def gain_copy(owner, to):
+        row = gains.at[owner]
+        return remote(row, row, gain_send.at[to], gain_recv.at[owner], a * blocks + to)
+
+    def gath_copy(t, base, u, theirs):
+        digit = (b >> t) & 1
+        held = 1 - digit if theirs else digit
+        index = u * (1 << (t + 1)) + held * (1 << t) + b % (1 << t)
+        lines = gath.at[lines_of(index), :]
+        partner = me + (1 - 2 * digit) * (1 << t)
+        return index, remote(lines, lines, ga_send.at[base + u], ga_recv.at[base + u], partner)
+
+    def turn(index):
+        if shard % 128 == 0:
+            norm_t[:, lines_of(index)] = gath[lines_of(index), :].T
+
+    gath[lines_of(b), :] = tok_ref[...]
+    gains[b] = jnp.broadcast_to(gain_ref[...], gains.shape[1:])
     values = tok_ref[...].astype(F32)
     ssq[me] = jnp.sum((values * values).reshape(shard // 8, 8, rows), axis=0)
     pl.semaphore_wait(barrier, count - 1)
 
-    def sq_copy(owner, to):
-        return remote(ssq.at[owner], ssq.at[owner], sq_send.at[to], sq_recv.at[owner], to)
-
     @pl.loop(1, count)
     def _(j):
         sq_copy(me, (me + j) % count).start()
+
+    @pl.loop(1, blocks)
+    def _(j):
+        gain_copy(b, (b + j) % blocks).start()
+
+    for t, base, many in plan:
+        gath_copy(t, base, b >> (t + 1), False)[1].start()
+
+    acc[...] = jnp.zeros_like(acc)
+    pending = [b]
+    for t, base, many in plan:
+        own = b >> (t + 1)
+        for j in range(1, many):
+            gath_copy(t, base, (own + j) % many, False)[1].start()
+        for index in pending:
+            turn(index)
+        pending = []
+        for u in range(many):
+            index, copy = gath_copy(t, base, u, True)
+            copy.wait_recv()
+            pending.append(index)
+    for index in pending:
+        turn(index)
+    if shard % 128 != 0:
+        norm_t[...] = gath[...].T
 
     @pl.loop(1, count)
     def _(j):
         other = (me + j) % count
         sq_copy(other, other).wait_recv()
 
+    @pl.loop(1, blocks)
+    def _(j):
+        other = (b + j) % blocks
+        gain_copy(other, other).wait_recv()
+
     squares = jnp.sum(jnp.sum(ssq[...], axis=0), axis=0, keepdims=True)
     inverse = lax.rsqrt(squares / (shard * count) + 1e-05)
-    normed = (values * inverse * gain_ref[...].astype(F32)).astype(BF16)
-
-    def lines_of(index):
-        return pl.ds(pl.multiple_of(index * shard, shard), shard)
-
-    gath[lines_of(b), :] = normed
-
-    def gath_copy(owner, to):
-        lines = gath.at[lines_of(owner), :]
-        return remote(lines, lines, ga_send.at[to], ga_recv.at[owner], a * blocks + to)
-
-    @pl.loop(1, blocks)
-    def _(j):
-        gath_copy(b, (b + j) % blocks).start()
-
-    acc[...] = jnp.zeros_like(acc)
-
-    @pl.loop(1, count)
-    def _(j):
-        sq_copy(me, (me + j) % count).wait_send()
-
-    @pl.loop(1, blocks)
-    def _(j):
-        other = (b + j) % blocks
-        gath_copy(other, other).wait_recv()
-
-    @pl.loop(1, blocks)
-    def _(j):
-        gath_copy(b, (b + j) % blocks).wait_send()
-
-    for at in range(0, width, 256):
-        norm_t[:, at : at + 256] = gath[at : at + 256, :].T
-
-    @pl.loop(0, steps + 2 * last * SKEW)
+    column = jnp.broadcast_to(inverse, (128, rows)).T[:, :1]
+    for q in range(blocks):
+        lanes = slice(q * shard, (q + 1) * shard)
+        norm_t[:, lanes] = (norm_t[:, lanes].astype(F32) * column * gains[q, :1, :]).astype(BF16)
+
+    @pl.loop(0, steps + last * (SKEW + BACK))
     def _(i):
         for d in range(2):
             r = roles[d]
-            k = i - SKEW * (last + last - r)
+            k = i - SKEW * last - BACK * (last - r)
 
             @pl.when((k >= 0) & (k < steps) & (r < last))
             def _(d=d, r=r, k=k):
@@ -219,7 +251,7 @@
 
         for d in range(2):
             r = roles[d]
-            k = i - SKEW * (last + last - r)
+            k = i - SKEW * last - BACK * (last - r)
 
             @pl.when((k >= 0) & (k < steps))
             def _(d=d, r=r, k=k):
@@ -231,8 +263,6 @@
                     down_copy(d, k + 1, 1 - slot).start()
 
                 acc[...] += jnp.dot(hid[d, k], wdn[d, slot], preferred_element_type=F32)
-
-    bits = blocks.bit_length() - 1
 
     def flipped(t):
         return (b >> t) & 1
@@ -278,6 +308,18 @@
         base += many
     out_ref[...] = final[lines_of(b), :].astype(BF16)
 
+    @pl.loop(1, count)
+    def _(j):
+        sq_copy(me, (me + j) % count).wait_send()
+
+    @pl.loop(1, blocks)
+    def _(j):
+        gain_copy(b, (b + j) % blocks).wait_send()
+
+    for t, base, many in plan:
+        for u in range(many):
+            gath_copy(t, base, u, False)[1].wait_send()
+
     for d in range(2):
         r = roles[d]
 
@@ -308,6 +350,7 @@
         out_specs=vmem,
         scratch_shapes=[
             pltpu.VMEM((count, 8, rows), F32),
+            pltpu.VMEM((blocks, 8, shard), F32),
             pltpu.VMEM((width, rows), BF16),
             pltpu.VMEM((rows, width), BF16),
             pltpu.VMEM((rows, 2 * CHUNK), F32),
@@ -321,6 +364,8 @@
             pltpu.VMEM((blocks - 1, shard, rows), BF16),
             dma((count,)),
             dma((count,)),
+            dma((blocks,)),
+            dma((blocks,)),
             dma((blocks,)),
             dma((blocks,)),
             dma((2, steps)),
@@ -341,7 +386,7 @@
             bytes_accessed=6 * width * gate_weight.shape[2],
             transcendentals=0,
         ),
-    )(tokens, norm_gain[:, None], gate_weight, up_weight, down_weight)
+    )(tokens, norm_gain.astype(F32)[None, :], gate_weight, up_weight, down_weight)
 
 
 def solution(mesh):

time: 276 us -> 269 us (0.975)
  Pallas kernels: 273 us -> 266 us
    pallas_call x1, Pallas kernels: 273 us -> 266 us  [shards(): pl.pallas_call(functools.partial(kernel, count), out_shape=jax.ShapeDtype...]
where the time goes in v2:
time: 269 us
  Pallas kernels  266 us (99%)
    pallas_call x1, Pallas kernels, shards(): pl.pallas_call(functools.partial(kernel, count), out_shape=jax.ShapeDtype...  266 us

profile of v2, /device:TPU:0, one launch (start us, length us, event | category | flops | bytes accessed | tf_op | source)
XLA Modules:
  0.0 268.9 jit_solution(7753442159446554164)
XLA Ops:
  0.0 1.3 broadcast_in_dim.7
  1.3 265.8 %shard_map.55 = bf16[512,384]{1,0:T(8,128)(2,1)} custom-call(bf16[512,384]{1,0:T(8,128)(2,1)} %tok_ref.1, f32[1,512]{1,0:T(1,128)} %bitcast.1, bf16[1,2048,8192]{2,1,0:T(8,128)(2,1)} %gate_ref.1, bf16[1,2048,8192]{2,1,0:T(8,128)(2,1)} %up_ref.1, bf16[1,8192,2048]{2,1,0:T(8,128)(2,1)} %down_ref.1), custom_call_target="tpu_custom_call" | custom-call | flops 38654705664 | bytes 100663296 | tf_op jit(solution)/shard_map/pallas_call | solution.py:346
  267.1 1.8 copy.7

commit v3 on v2

--- a/solution.py
+++ b/solution.py
@@ -199,18 +199,6 @@
     def _(i):
         for d in range(2):
             r = roles[d]
-            k = i - SKEW * last - BACK * (last - r)
-
-            @pl.when((k >= 0) & (k < steps) & (r < last))
-            def _(d=d, r=r, k=k):
-                hid_copy(d, k).wait_recv()
-
-                @pl.when(r > 0)
-                def _():
-                    hid_copy(d, k).start()
-
-        for d in range(2):
-            r = roles[d]
             k = i - SKEW * r
 
             @pl.when((k >= 0) & (k < steps))
@@ -247,6 +235,18 @@
                     total = part[...] + red[d, k].astype(F32)
                     gate = total[:, :CHUNK]
                     hid[d, k] = (gate / (1.0 + jnp.exp(-gate)) * total[:, CHUNK:]).astype(BF16)
+                    hid_copy(d, k).start()
+
+        for d in range(2):
+            r = roles[d]
+            k = i - SKEW * last - BACK * (last - r)
+
+            @pl.when((k >= 0) & (k < steps) & (r < last))
+            def _(d=d, r=r, k=k):
+                hid_copy(d, k).wait_recv()
+
+                @pl.when(r > 0)
+                def _():
                     hid_copy(d, k).start()
 
         for d in range(2):

time: 269 us -> 269 us (level)
  no operation moved by 1% of the time
where the time goes in v3:
time: 269 us; the launch traced here: 268 us
  Pallas kernels  265 us (99%)
    pallas_call x1, Pallas kernels, shards(): pl.pallas_call(functools.partial(kernel, count), out_shape=jax.ShapeDtype...  265 us

profile of v3, /device:TPU:0, one launch (start us, length us, event | category | flops | bytes accessed | tf_op | source)
XLA Modules:
  0.0 268.3 jit_solution(2574078428729334627)
XLA Ops:
  0.0 1.3 broadcast_in_dim.7
  1.3 265.2 %shard_map.55 = bf16[512,384]{1,0:T(8,128)(2,1)} custom-call(bf16[512,384]{1,0:T(8,128)(2,1)} %tok_ref.1, f32[1,512]{1,0:T(1,128)} %bitcast.1, bf16[1,2048,8192]{2,1,0:T(8,128)(2,1)} %gate_ref.1, bf16[1,2048,8192]{2,1,0:T(8,128)(2,1)} %up_ref.1, bf16[1,8192,2048]{2,1,0:T(8,128)(2,1)} %down_ref.1), custom_call_target="tpu_custom_call" | custom-call | flops 38654705664 | bytes 100663296 | tf_op jit(solution)/shard_map/pallas_call | solution.py:346
  266.5 1.8 copy.7
